TPU v7x, 32 devices: a whole 2x2x4 slice. The times are simulated.
32 devices in a mesh: grp: 2 (over x), seq: 16 (over z, y, core).
Axes of the slice: x: 2, y: 2, z: 4, core: 2. Of those that a mesh axis runs over, the one named last changes fastest.
Arguments:
- tokens: bfloat16 [16384, 1024], P(('grp', 'seq')), may hold values from -20 to 20
- qkv_weight: bfloat16 [1024, 1536], replicated, may hold values from -2 to 2
- cov_embed: bfloat16 [64, 1024], P(('grp', 'seq')), may hold values from -20 to 20
- cov_slot: int32 [32], replicated, may hold values from 0 to 63, as said below
- block_links: int32 [128, 2], P(('grp', 'seq')), may hold values from 0 to 1, as said below
Outputs:
- attended: bfloat16 [16384, 512], P(('grp', 'seq'))
Inputs may be any that keep to these rules, and one draw needn't show every extreme that they name: The values are distinct; covariate c is held in slot cov_slot[c], on the device that holds that row of cov_embed. block_links[b, 1] equals block_links[b + 1, 0]; block_links[0, 0] and block_links[127, 1] are 0.
All inputs are finite; a program needn't handle non-finite values.
Results may differ from a plain program's by a relative error of at most 0.0015.
The roundings to bfloat16 on the way count: a program that leaves them out, or rounds other values in their place, can miss the bound.
Values may be sent and summed in bfloat16 or wider, within the bound.
A program may use at most 64 MiB of HBM per device.

v0:
```python
import math
import jax
import jax.numpy as jnp
from jax import lax
from jax.sharding import PartitionSpec as P

HEADS = 8
BLOCK = 128
masked_score = -1e30


def extended(cells, sides, width):
    for axis, dim in sides:
        count = lax.axis_size(axis)
        ends = count - 1
        head = lax.slice_in_dim(cells, 0, width, axis=dim)
        tail = lax.slice_in_dim(cells, cells.shape[dim] - width, cells.shape[dim], axis=dim)
        cells = jnp.concatenate(
            [
                lax.ppermute(tail, axis, [(i, (i + 1) % count) for i in range(ends)]),
                cells,
                lax.ppermute(head, axis, [((i + 1) % count, i) for i in range(ends)]),
            ],
            axis=dim,
        )
    return cells


def window_attend(queries, before, middle, after, left_open, right_open, cov_kv, head_count):
    blocks, block_rows, attn_width = queries.shape
    head_width = attn_width // head_count
    score_scale = 1.0 / math.sqrt(head_width)
    query_heads = queries.reshape(blocks, block_rows, head_count, head_width)

    def divide_parts(joined):
        key_part = joined[:, :, :attn_width].reshape(blocks, block_rows, head_count, head_width)
        value_part = joined[:, :, attn_width:].reshape(blocks, block_rows, head_count, head_width)
        return (key_part, value_part)

    key_before, value_before = divide_parts(before)
    key_middle, value_middle = divide_parts(middle)
    key_after, value_after = divide_parts(after)
    cov_count = cov_kv.shape[0]
    cov_keys = cov_kv[:, :attn_width].reshape(cov_count, head_count, head_width)
    cov_values = cov_kv[:, attn_width:].reshape(cov_count, head_count, head_width)

    def local_scores(key_part):
        return (
            jnp.einsum("nqhd,nkhd->nqhk", query_heads, key_part, preferred_element_type=jnp.float32)
            * score_scale
        )

    score_before = jnp.where(
        (left_open > 0)[:, None, None, None], local_scores(key_before), masked_score
    )
    score_middle = local_scores(key_middle)
    score_after = jnp.where(
        (right_open > 0)[:, None, None, None], local_scores(key_after), masked_score
    )
    score_global = (
        jnp.einsum("nqhd,chd->nqhc", query_heads, cov_keys, preferred_element_type=jnp.float32)
        * score_scale
    )
    highest = jnp.maximum(
        jnp.maximum(
            jnp.max(score_before, axis=-1, keepdims=True),
            jnp.max(score_middle, axis=-1, keepdims=True),
        ),
        jnp.maximum(
            jnp.max(score_after, axis=-1, keepdims=True),
            jnp.max(score_global, axis=-1, keepdims=True),
        ),
    )
    weight_before = jnp.exp(score_before - highest)
    weight_middle = jnp.exp(score_middle - highest)
    weight_after = jnp.exp(score_after - highest)
    weight_global = jnp.exp(score_global - highest)
    denominator = (
        jnp.sum(weight_before, axis=-1)
        + jnp.sum(weight_middle, axis=-1)
        + jnp.sum(weight_after, axis=-1)
        + jnp.sum(weight_global, axis=-1)
    )

    def local_values(weights, value_part):
        return jnp.einsum(
            "nqhk,nkhd->nqhd",
            weights.astype(jnp.bfloat16),
            value_part,
            preferred_element_type=jnp.float32,
        )

    summed = local_values(weight_before, value_before) + local_values(weight_middle, value_middle)
    summed = summed + local_values(weight_after, value_after)
    summed = summed + jnp.einsum(
        "nqhc,chd->nqhd",
        weight_global.astype(jnp.bfloat16),
        cov_values,
        preferred_element_type=jnp.float32,
    )
    result = (summed / denominator[..., None]).astype(jnp.bfloat16)
    return result.reshape(blocks * block_rows, attn_width)


def local(tokens, qkv_weight, cov_embed, cov_slot, block_links):
    tok_rows = tokens.shape[0]
    attn_width = qkv_weight.shape[1] // 3
    block_rows = BLOCK
    blocks = tok_rows // block_rows
    projected = jnp.dot(tokens, qkv_weight, preferred_element_type=jnp.float32).astype(jnp.bfloat16)
    queries = projected[:, :attn_width]
    keyvalue = projected[:, attn_width:]
    padded = extended(keyvalue, ((("grp", "seq"), 0),), block_rows)
    value_weight = qkv_weight[:, attn_width:]
    every_row = lax.all_gather(cov_embed, ("grp", "seq"), axis=0, tiled=True)
    chosen = jnp.take(every_row, cov_slot, axis=0)
    cov_kv = jnp.dot(chosen, value_weight, preferred_element_type=jnp.float32).astype(jnp.bfloat16)
    before = padded[:tok_rows].reshape(blocks, block_rows, 2 * attn_width)
    middle = keyvalue.reshape(blocks, block_rows, 2 * attn_width)
    after = padded[2 * block_rows : 2 * block_rows + tok_rows].reshape(
        blocks, block_rows, 2 * attn_width
    )
    return window_attend(
        queries.reshape(blocks, block_rows, attn_width),
        before,
        middle,
        after,
        block_links[:, 0],
        block_links[:, 1],
        cov_kv,
        HEADS,
    )


def solution(mesh):
    placed = (P(("grp", "seq"), None), P(), P(("grp", "seq"), None), P(), P(("grp", "seq"), None))
    return jax.shard_map(
        local, mesh=mesh, in_specs=placed, out_specs=P(("grp", "seq"), None), check_vma=False
    )
```

profile of v0, /device:TPU:0, one launch (start us, length us, event | category | flops | bytes accessed | tf_op | source)
XLA Modules:
  0.0 99.4 jit_solution(9266033365159456441)
XLA Ops:
  0.0 0.0 copy-start
  0.0 1.2 %copy-done = bf16[512,1024]{1,0:T(8,128)(2,1)S(1)} copy-done((bf16[512,1024]{1,0:T(8,128)(2,1)S(1)}, bf16[512,1024]{1,0:T(8,128)(2,1)}, u32[]{:S(2)}) %copy-start) | copy-done | bytes 1048600
  1.2 3.7 %convolution_convert_fusion = bf16[512,1536]{1,0:T(8,128)(2,1)S(1)} fusion(bf16[512,1024]{1,0:T(8,128)(2,1)S(1)} %copy-done, bf16[1024,1536]{1,0:T(8,128)(2,1)} %param.6), kind=kOutput, calls=%fused_computation.1 | convolution fusion | flops 1611399168 | bytes 5767168 | tf_op jit(solution)/shard_map/dot_general | solution.py:110
  4.9 0.0 copy-start.15
  4.9 0.9 fusion.56
  5.8 2.4 %collective-permute-start = (bf16[128,1024]{1,0:T(8,128)(2,1)}, bf16[128,1024]{1,0:T(8,128)(2,1)S(1)}, u32[]{:S(2)}, u32[]{:S(2)}) collective-permute-start(bf16[128,1024]{1,0:T(8,128)(2,1)} %get-tuple-element.8), channel_id=1, source_target_pairs={{0,1},{1,2},{2,3},{3,4},{4,5},{5,6},{6,7},{7,8},{8,9},{9,10},{10,1... | collective-permute-start | bytes 786440 | tf_op jit(solution)/shard_map/ppermute | solution.py:20
  8.1 1.3 %collective-permute-start.1 = (bf16[128,1024]{1,0:T(8,128)(2,1)}, bf16[128,1024]{1,0:T(8,128)(2,1)}, u32[]{:S(2)}, u32[]{:S(2)}) collective-permute-start(bf16[128,1024]{1,0:T(8,128)(2,1)} %get-tuple-element.9), channel_id=1, source_target_pairs={{1,0},{2,1},{3,2},{4,3},{5,4},{6,5},{7,6},{8,7},{9,8},{10,9},{11,1... | collective-permute-start | bytes 786440 | tf_op jit(solution)/shard_map/ppermute | solution.py:22
  9.4 0.1 slice.75
  9.6 0.0 copy-start.3
  9.6 0.0 copy-done.15
  9.7 0.2 copy.66
  9.9 0.0 copy-start.13
  9.9 0.9 reshape_reshape.3
  10.8 0.9 fusion.58
  11.7 0.0 copy-done.3
  11.7 1.0 %copy.68 = bf16[4,128,512]{1,2,0:T(8,128)(2,1)} copy(bf16[4,128,512]{2,1,0:T(8,128)(2,1)S(1)} %get-tuple-element.13) | data formatting | bytes 1048576 | tf_op jit(solution)/shard_map/slice | solution.py:36
  12.7 0.0 copy-done.13
  12.7 45.4 %all-gather = bf16[32,2,1024]{2,1,0:T(2,128)(2,1)S(1)} all-gather(bf16[1,2,1024]{2,1,0:T(2,128)(2,1)S(1)} %bitcast.82), channel_id=1, replica_groups=mesh['grp'=2,'seq'=16] {'grp','seq'}, dimensions={0}, use_global_device_ids=true | all-gather | bytes 135168 | tf_op jit(solution)/shard_map/all_gather | solution.py:115
  58.2 0.1 reshape.102
  58.3 0.6 gather_fusion
  58.9 0.0 copy-start.7
  58.9 2.2 %fusion.16 = bf16[32,1024]{1,0:T(8,128)(2,1)S(1)} fusion(bf16[1024,1536]{1,0:T(8,128)(2,1)} %param.6, bf16[32,1024]{1,0:T(8,128)(2,1)S(1)} %gather_fusion, pred[32]{0:T(512)(128)(4,1)S(1)} %compare_and_fusion), kind=kOutput, calls=%fused_computation.30 | convolution fusion | flops 67174400 | bytes 2228256 | tf_op jit(solution)/shard_map/dot_general | solution.py:117
  61.1 0.0 copy-start.14
  61.1 0.6 fusion.60
  61.7 0.0 copy-done.7
  61.7 1.6 %bitcast_reduce_fusion.1 = (f32[4,128,8]{1,2,0:T(8,128)S(1)}, f32[4,8,128,128]{3,2,1,0:T(8,128)S(1)}) fusion(bf16[4,128,8,64]{1,3,2,0:T(8,128)(2,1)S(1)} %bitcast.76, bf16[4,128,8,64]{1,0,3,2:T(4,128)(2,1)} %reshape_reshape.3), kind=kOutput, calls=%fused_computation.6 | convolution fusion | flops 68153344 | bytes 3162112 | tf_op jit(solution)/shard_map/nqhd,nkhd->nqhk/dot_general | solution.py:49
  63.3 0.0 copy-done.14
  63.3 0.5 compare_bitcast_fusion.1
  63.8 0.1 reshape.87
  63.9 2.0 %copy.76 = bf16[4,128,512]{1,2,0:T(8,128)(2,1)} copy(bf16[4,128,512]{2,1,0:T(8,128)(2,1)} %get-tuple-element.12) | data formatting | bytes 1048576 | tf_op jit(solution)/shard_map/slice | solution.py:37
  66.0 0.9 reshape.90
  66.8 2.7 %fusion.61 = (f32[4,128,8]{1,0,2:T(4,128)}, f32[4,128,8,32]{1,3,0,2:T(8,128)}) fusion(bf16[4,128,8,64]{1,0,3,2:T(4,128)(2,1)} %reshape_reshape.3, bf16[32,8,64,1]{2,1,0,3:T(8,128)(2,1)S(1)} %bitcast.81), kind=kOutput, calls=%fused_computation.80 | convolution fusion | flops 17035264 | bytes 1097728 | tf_op jit(solution)/shard_map/nqhd,chd->nqhc/dot_general | solution.py:61
  69.5 0.0 collective-permute-done
  69.5 0.0 collective-permute-done.1
  69.5 2.6 %pad_maximum_fusion.1 = (bf16[512,1024]{1,0:T(8,128)(2,1)S(1)}, bf16[512,1024]{1,0:T(8,128)(2,1)}) fusion(bf16[512,1024]{1,0:T(8,128)(2,1)} %copy-done.3, bf16[128,1024]{1,0:T(8,128)(2,1)S(1)} %collective-permute-done, bf16[128,1024]{1,0:T(8,128)(2,1)} %collective-permute-done.1), kind=kLoop, calls=%fused_computation.33 | loop fusion | flops 4194304 | bytes 3670016 | tf_op jit(solution)/shard_map/concatenate | solution.py:18
  72.1 1.1 %fusion.59 = (bf16[4,128,512]{2,1,0:T(8,128)(2,1)}, bf16[4,128,512]{2,1,0:T(8,128)(2,1)}) fusion(bf16[4,128,1024]{2,1,0:T(8,128)(2,1)S(1)} %bitcast.74), kind=kLoop, calls=%fused_computation.78 | loop fusion | bytes 2097152 | tf_op jit(solution)/shard_map/slice | solution.py:37
  73.2 2.0 %copy.65 = bf16[4,128,512]{1,2,0:T(8,128)(2,1)} copy(bf16[4,128,512]{2,1,0:T(8,128)(2,1)} %get-tuple-element.15) | data formatting | bytes 1048576 | tf_op jit(solution)/shard_map/slice | solution.py:36
  75.3 2.3 %fusion.57 = (bf16[4,128,512]{2,1,0:T(8,128)(2,1)}, bf16[4,128,512]{2,1,0:T(8,128)(2,1)}) fusion(bf16[4,128,1024]{2,1,0:T(8,128)(2,1)} %bitcast.73), kind=kLoop, calls=%fused_computation.76 | loop fusion | bytes 2097152 | tf_op jit(solution)/shard_map/slice | solution.py:37
  77.5 2.1 %copy.70 = bf16[4,128,512]{1,2,0:T(8,128)(2,1)} copy(bf16[4,128,512]{2,1,0:T(8,128)(2,1)} %get-tuple-element.11) | data formatting | bytes 1048576 | tf_op jit(solution)/shard_map/slice | solution.py:36
  79.6 0.0 copy-done.11
  79.6 3.3 %bitcast_reduce_fusion.2 = (f32[4,128,8]{1,2,0:T(8,128)S(1)}, f32[4,8,128,128]{3,2,1,0:T(8,128)}) fusion(pred[4]{0:T(512)(128)(4,1)S(1)} %copy-done.11, bf16[4,128,8,64]{1,3,2,0:T(8,128)(2,1)} %bitcast.77, bf16[4,128,8,64]{1,0,3,2:T(4,128)(2,1)} %reshape_reshape.3), kind=kOutput, calls=%fused_computation.9 | convolution fusion | flops 68677632 | bytes 3162116 | tf_op jit(solution)/shard_map/nqhd,nkhd->nqhk/dot_general | solution.py:49
  82.9 0.0 copy-done.12
  82.9 0.0 copy-done.2
  82.9 0.0 copy-done.8
  82.9 2.0 %bitcast_reduce_fusion = (f32[4,128,8]{1,2,0:T(8,128)S(1)}, f32[4,8,128,128]{3,2,1,0:T(8,128)}) fusion(pred[4]{0:T(512)(128)(4,1)S(1)} %copy-done.12, bf16[4,128,8,64]{1,3,2,0:T(8,128)(2,1)S(1)} %bitcast.78, bf16[4,128,8,64]{1,0,3,2:T(4,128)(2,1)S(1)} %copy-done.2), kind=kOutput, calls=%fused_computation.3 | convolution fusion | flops 68677632 | bytes 3162116 | tf_op jit(solution)/shard_map/nqhd,nkhd->nqhk/dot_general | solution.py:49
  84.8 0.0 copy-done.10
  84.9 2.0 %copy.64 = bf16[4,128,512]{1,2,0:T(8,128)(2,1)} copy(bf16[4,128,512]{2,1,0:T(8,128)(2,1)} %get-tuple-element.14) | data formatting | bytes 1048576 | tf_op jit(solution)/shard_map/slice | solution.py:37
  86.9 2.1 %copy.78 = bf16[4,128,512]{1,2,0:T(8,128)(2,1)} copy(bf16[4,128,512]{2,1,0:T(8,128)(2,1)} %get-tuple-element.10) | data formatting | bytes 1048576 | tf_op jit(solution)/shard_map/slice | solution.py:37
  89.0 2.6 %fusion.20 = f32[4,8,64,128]{3,2,1,0:T(8,128)S(1)} fusion(bf16[4,128,8,64]{1,3,2,0:T(8,128)(2,1)} %bitcast.79, f32[4,8,128,128]{3,2,1,0:T(8,128)} %get-tuple-element.29, f32[4,128,8]{1,2,0:T(8,128)S(1)} %fusion.49, pred[4]{0:T(512)(128)(4,1)S(1)} %copy-done.11), kind=kOutput, calls=%fused_computation.31 | convolution fusion | flops 69206016 | bytes 3686404 | tf_op jit(solution)/shard_map/nqhk,nkhd->nqhd/dot_general | solution.py:86
  91.6 0.0 copy-done.1
  91.6 0.0 copy-start.6
  91.6 0.0 copy-start.5
  91.6 3.2 %fusion.5 = (f32[4,128,8]{1,2,0:T(8,128)S(1)}, f32[4,128,8]{1,2,0:T(8,128)S(1)}, f32[4,128,8]{1,2,0:T(8,128)S(1)}) fusion(f32[4,8,128,128]{3,2,1,0:T(8,128)S(1)} %get-tuple-element.31, f32[4,128,8]{1,2,0:T(8,128)S(1)} %fusion.49, f32[4,8,128,128]{3,2,1,0:T(8,128)S(1)} %copy-done.1, pred[4]{0:T(512)(128)(4,1)S(1)} %copy-done.11, ...), kind=kLoop, calls=%fused_computation.15 | loop fusion | flops 5754880 | bytes 6357000 | tf_op jit(solution)/shard_map/reduce_sum | solution.py:80
  94.8 0.0 copy-done.6
  94.8 0.1 fusion.34
  95.0 0.0 copy-done.5
  95.0 0.0 copy-start.4
  95.0 0.5 convolution_add_fusion.1
  95.5 0.3 convolution_bitcast_fusion
  95.9 0.7 copy-done.4
  96.6 0.1 copy-done.9
  96.7 0.8 fusion.14
  97.5 0.6 copy.92
  98.0 1.4 %reshape.105 = bf16[512,512]{1,0:T(8,128)(2,1)} reshape(bf16[4,128,8,64]{3,2,1,0:T(8,128)(2,1)S(1)} %copy.92) | data formatting | bytes 1048576 | tf_op jit(solution)/shard_map/reshape | solution.py:102
  (14 shorter events, 0.1 us)
Async XLA Ops:
  0.0 1.2 %copy-start = (bf16[512,1024]{1,0:T(8,128)(2,1)S(1)}, bf16[512,1024]{1,0:T(8,128)(2,1)}, u32[]{:S(2)}) copy-start(bf16[512,1024]{1,0:T(8,128)(2,1)} %param.5) | copy-start | bytes 3145732
  4.9 4.7 %copy-start.15 = (s32[32]{0:T(128)S(1)}, s32[32]{0:T(128)}, u32[]{:S(2)}) copy-start(s32[32]{0:T(128)} %param.8) | copy-start | bytes 388
  5.8 63.7 %collective-permute-start = (bf16[128,1024]{1,0:T(8,128)(2,1)}, bf16[128,1024]{1,0:T(8,128)(2,1)S(1)}, u32[]{:S(2)}, u32[]{:S(2)}) collective-permute-start(bf16[128,1024]{1,0:T(8,128)(2,1)} %get-tuple-element.8), channel_id=1, source_target_pairs={{0,1},{1,2},{2,3},{3,4},{4,5},{5,6},{6,7},{7,8},{8,9},{9,10},{10,1... | collective-permute-start | bytes 786440 | tf_op jit(solution)/shard_map/ppermute | solution.py:20
  8.1 61.4 %collective-permute-start.1 = (bf16[128,1024]{1,0:T(8,128)(2,1)}, bf16[128,1024]{1,0:T(8,128)(2,1)}, u32[]{:S(2)}, u32[]{:S(2)}) collective-permute-start(bf16[128,1024]{1,0:T(8,128)(2,1)} %get-tuple-element.9), channel_id=1, source_target_pairs={{1,0},{2,1},{3,2},{4,3},{5,4},{6,5},{7,6},{8,7},{9,8},{10,9},{11,1... | collective-permute-start | bytes 786440 | tf_op jit(solution)/shard_map/ppermute | solution.py:22
  9.6 2.2 %copy-start.3 = (bf16[512,1024]{1,0:T(8,128)(2,1)}, bf16[512,1024]{1,0:T(8,128)(2,1)S(1)}, u32[]{:S(2)}) copy-start(bf16[512,1024]{1,0:T(8,128)(2,1)S(1)} %slice.75) | copy-start | bytes 3145732
  9.9 2.8 %copy-start.13 = (bf16[2,1024]{1,0:T(2,128)(2,1)S(1)}, bf16[2,1024]{1,0:T(2,128)(2,1)}, u32[]{:S(2)}) copy-start(bf16[2,1024]{1,0:T(2,128)(2,1)} %param.7) | copy-start | bytes 12292
  58.9 2.8 %copy-start.7 = (bf16[4,128,512]{1,2,0:T(8,128)(2,1)S(1)}, bf16[4,128,512]{1,2,0:T(8,128)(2,1)}, u32[]{:S(2)}) copy-start(bf16[4,128,512]{1,2,0:T(8,128)(2,1)} %copy.68) | copy-start | bytes 1572868
  61.1 2.2 %copy-start.14 = (s32[4,2]{0,1:T(2,128)S(1)}, s32[4,2]{0,1:T(2,128)}, u32[]{:S(2)}) copy-start(s32[4,2]{0,1:T(2,128)} %param.9) | copy-start | bytes 100
  73.2 6.4 %copy-start.11 = (pred[4]{0:T(512)(128)(4,1)S(1)}, pred[4]{0:T(512)(128)(4,1)}, u32[]{:S(2)}) copy-start(pred[4]{0:T(512)(128)(4,1)} %get-tuple-element.22) | copy-start | bytes 16
  77.5 5.3 %copy-start.12 = (pred[4]{0:T(512)(128)(4,1)S(1)}, pred[4]{0:T(512)(128)(4,1)}, u32[]{:S(2)}) copy-start(pred[4]{0:T(512)(128)(4,1)} %get-tuple-element.23) | copy-start | bytes 16
  79.6 3.3 %copy-start.2 = (bf16[4,128,8,64]{1,0,3,2:T(4,128)(2,1)S(1)}, bf16[4,128,8,64]{1,0,3,2:T(4,128)(2,1)}, u32[]{:S(2)}) copy-start(bf16[4,128,8,64]{1,0,3,2:T(4,128)(2,1)} %reshape_reshape.3) | copy-start | bytes 1572868
  79.6 3.3 %copy-start.8 = (bf16[4,128,512]{1,2,0:T(8,128)(2,1)S(1)}, bf16[4,128,512]{1,2,0:T(8,128)(2,1)}, u32[]{:S(2)}) copy-start(bf16[4,128,512]{1,2,0:T(8,128)(2,1)} %copy.70) | copy-start | bytes 1572868
  82.9 2.0 %copy-start.10 = (f32[4,128,8]{1,0,2:T(4,128)S(1)}, f32[4,128,8]{1,0,2:T(4,128)}, u32[]{:S(2)}) copy-start(f32[4,128,8]{1,0,2:T(4,128)} %get-tuple-element.26) | copy-start | bytes 49156
  89.0 2.6 %copy-start.1 = (f32[4,8,128,128]{3,2,1,0:T(8,128)S(1)}, f32[4,8,128,128]{3,2,1,0:T(8,128)}, u32[]{:S(2)}) copy-start(f32[4,8,128,128]{3,2,1,0:T(8,128)} %get-tuple-element.29) | copy-start | bytes 6291460
  91.6 3.2 %copy-start.6 = (f32[4,128,8,32]{1,3,0,2:T(8,128)S(1)}, f32[4,128,8,32]{1,3,0,2:T(8,128)}, u32[]{:S(2)}) copy-start(f32[4,128,8,32]{1,3,0,2:T(8,128)} %get-tuple-element.27) | copy-start | bytes 1572868
  91.6 3.4 %copy-start.5 = (bf16[4,128,512]{1,2,0:T(8,128)(2,1)S(1)}, bf16[4,128,512]{1,2,0:T(8,128)(2,1)}, u32[]{:S(2)}) copy-start(bf16[4,128,512]{1,2,0:T(8,128)(2,1)} %copy.76) | copy-start | bytes 1572868
  95.0 1.6 %copy-start.4 = (f32[4,8,128,128]{3,2,1,0:T(8,128)S(1)}, f32[4,8,128,128]{3,2,1,0:T(8,128)}, u32[]{:S(2)}) copy-start(f32[4,8,128,128]{3,2,1,0:T(8,128)} %get-tuple-element.25) | copy-start | bytes 6291460
  95.0 1.7 %copy-start.9 = (bf16[4,128,512]{1,2,0:T(8,128)(2,1)S(1)}, bf16[4,128,512]{1,2,0:T(8,128)(2,1)}, u32[]{:S(2)}) copy-start(bf16[4,128,512]{1,2,0:T(8,128)(2,1)} %copy.78) | copy-start | bytes 1572868
where the time goes:
time: 100 us; the launch traced here: 99.4 us
  blocking collectives  45.4 us (45%)
  local copies, waits for them, and re-layouts  24 us (24%)
  matrix products  19.6 us (20%)
  other arithmetic  6.55 us (7%)
  starting transfers between devices  3.65 us (4%)
    all_gather x1, blocking collectives, local(): every_row = lax.all_gather(cov_embed, ('grp', 'seq'), axis=0, tiled=True)  45.4 us
    slice x6, local copies, waits for them, and re-layouts, divide_parts(): joined[:, :, attn_width:]  10.4 us
    dot_general x3, matrix products, local_scores(): jnp.einsum('nqhd,nkhd->nqhk', query_heads, key_part, preferred_element_ty...  6.79 us
    slice x3, local copies, waits for them, and re-layouts, divide_parts(): joined[:, :, :attn_width]  5.1 us
    dot_general x3, matrix products, local_values(): jnp.einsum('nqhk,nkhd->nqhd', weights.astype(jnp.bfloat16), value_part, p...  3.93 us
    dot_general x1, matrix products, local(): jnp.dot(tokens, qkv_weight, preferred_element_type=jnp.float32)  3.67 us
    reduce_sum x1, other arithmetic, window_attend(): jnp.sum(weight_middle, axis=-1)  3.2 us
    dot_general x1, matrix products, window_attend(): jnp.einsum('nqhd,chd->nqhc', query_heads, cov_keys, preferred_element_typ...  2.66 us
  transfers between devices with their start and end apart: 2, of which 0 were waited for; matrix products, arithmetic and copies ran while one was open for 15% of the time, Pallas kernels for 0%

commit v1 on v0

--- a/solution.py
+++ b/solution.py
@@ -1,12 +1,43 @@
+import functools
 import math
 import jax
 import jax.numpy as jnp
 from jax import lax
 from jax.sharding import PartitionSpec as P
+from jax.lax import axis_index, axis_size, ppermute
 
 HEADS = 8
 BLOCK = 128
 masked_score = -1e30
+
+
+def supply_the_rounds(z, row_dim):
+    mixed_arr = list(z.shape[1:])
+    mixed_arr[row_dim] *= z.shape[0]
+    return jnp.moveaxis(z, 0, row_dim).reshape(mixed_arr)
+
+
+def spots_register(chunk, row_axis):
+    o_now, y_new = (axis_size(row_axis), axis_index(row_axis))
+    raw_out, z1 = (chunk[None], 1)
+    while z1 < o_now:
+        buffer = []
+        for num in tuple(range(o_now)):
+            buffer.append((num, num ^ z1))
+        d_next = ppermute(raw_out, row_axis, buffer)
+        b_now = y_new & z1 == 0
+        raw_out = jnp.concatenate(
+            [jnp.where(b_now, raw_out, d_next), jnp.where(b_now, d_next, raw_out)]
+        )
+        z1 *= 2
+    return raw_out
+
+
+def launch_values(z_in, arr_in, array_axis):
+    return supply_the_rounds(spots_register(z_in, arr_in), array_axis)
+
+
+_derive_rates = functools.partial(launch_values, arr_in=("grp", "seq"), array_axis=0)
 
 
 def extended(cells, sides, width):
@@ -112,7 +143,7 @@
     keyvalue = projected[:, attn_width:]
     padded = extended(keyvalue, ((("grp", "seq"), 0),), block_rows)
     value_weight = qkv_weight[:, attn_width:]
-    every_row = lax.all_gather(cov_embed, ("grp", "seq"), axis=0, tiled=True)
+    every_row = _derive_rates(cov_embed)
     chosen = jnp.take(every_row, cov_slot, axis=0)
     cov_kv = jnp.dot(chosen, value_weight, preferred_element_type=jnp.float32).astype(jnp.bfloat16)
     before = padded[:tok_rows].reshape(blocks, block_rows, 2 * attn_width)

time: 100 us -> 74.1 us (0.74)
  blocking collectives: 45.4 us -> 0 us
  starting transfers between devices: 3.65 us -> 19.6 us
  waiting for transfers between devices: 0.01 us -> 5.58 us
  local copies, waits for them, and re-layouts: 24 us -> 22.2 us
    all_gather x1 -> x0, blocking collectives: 45.4 us -> none  [local(): every_row = lax.all_gather(cov_embed, ('grp', 'seq'), axis=0, tiled=True)]
    ppermute x0 -> x5, starting transfers between devices: none -> 15.3 us  [spots_register(): d_next = ppermute(raw_out, row_axis, buffer)]
    ppermute x0 -> x5, waiting for transfers between devices: none -> 5.57 us  [spots_register(): d_next = ppermute(raw_out, row_axis, buffer)]
    unnamed x33 -> x24, local copies, waits for them, and re-layouts: 2.14 us -> 1.6 us
  transfers between devices with their start and end apart: 2 -> 7, of which waited for: 0 -> 3; matrix products, arithmetic and copies ran while one was open for 15% -> 24% of each run, Pallas kernels for 0% -> 0%
where the time goes in v1:
time: 74.1 us; the launch traced here: 73.5 us
  local copies, waits for them, and re-layouts  22.2 us (30%)
  starting transfers between devices  19.6 us (26%)
  matrix products  19 us (26%)
  other arithmetic  6.73 us (9%)
  waiting for transfers between devices  5.58 us (8%)
    ppermute x5, starting transfers between devices, spots_register(): d_next = ppermute(raw_out, row_axis, buffer)  15.3 us
    slice x6, local copies, waits for them, and re-layouts, divide_parts(): joined[:, :, attn_width:]  10.5 us
    dot_general x3, matrix products, local_scores(): jnp.einsum('nqhd,nkhd->nqhk', query_heads, key_part, preferred_element_ty...  6.93 us
    ppermute x5, waiting for transfers between devices, spots_register(): d_next = ppermute(raw_out, row_axis, buffer)  5.57 us
    slice x3, local copies, waits for them, and re-layouts, divide_parts(): joined[:, :, :attn_width]  5.13 us
    dot_general x3, matrix products, local_values(): jnp.einsum('nqhk,nkhd->nqhd', weights.astype(jnp.bfloat16), value_part, p...  3.93 us
    dot_general x1, matrix products, local(): jnp.dot(tokens, qkv_weight, preferred_element_type=jnp.float32)  3.67 us
    reduce_sum x1, other arithmetic, window_attend(): jnp.sum(weight_middle, axis=-1)  3.2 us
  transfers between devices with their start and end apart: 7, of which 3 were waited for; matrix products, arithmetic and copies ran while one was open for 24% of the time, Pallas kernels for 0%

profile of v1, /device:TPU:0, one launch (start us, length us, event | category | flops | bytes accessed | tf_op | source)
XLA Modules:
  0.0 73.5 jit_solution(7730554411755718641)
XLA Ops:
  0.0 0.0 copy-start
  0.0 0.5 collective-permute-start.2
  0.5 0.8 %copy-done = bf16[512,1024]{1,0:T(8,128)(2,1)S(1)} copy-done((bf16[512,1024]{1,0:T(8,128)(2,1)S(1)}, bf16[512,1024]{1,0:T(8,128)(2,1)}, u32[]{:S(2)}) %copy-start) | copy-done | bytes 1048600
  1.2 3.7 %convolution_convert_fusion = bf16[512,1536]{1,0:T(8,128)(2,1)S(1)} fusion(bf16[512,1024]{1,0:T(8,128)(2,1)S(1)} %copy-done, bf16[1024,1536]{1,0:T(8,128)(2,1)} %param.6), kind=kOutput, calls=%fused_computation.1 | convolution fusion | flops 1611399168 | bytes 5767168 | tf_op jit(solution)/shard_map/dot_general | solution.py:141
  4.9 0.9 %fusion.56 = (bf16[128,1024]{1,0:T(8,128)(2,1)}, bf16[128,1024]{1,0:T(8,128)(2,1)}) fusion(bf16[512,1536]{1,0:T(8,128)(2,1)S(1)} %convolution_convert_fusion), kind=kLoop, calls=%fused_computation.90 | loop fusion | bytes 1048576 | tf_op jit(solution)/shard_map/slice | solution.py:48
  5.8 3.0 %collective-permute-start = (bf16[128,1024]{1,0:T(8,128)(2,1)}, bf16[128,1024]{1,0:T(8,128)(2,1)}, u32[]{:S(2)}, u32[]{:S(2)}) collective-permute-start(bf16[128,1024]{1,0:T(8,128)(2,1)} %get-tuple-element.8), channel_id=1, source_target_pairs={{0,1},{1,2},{2,3},{3,4},{4,5},{5,6},{6,7},{7,8},{8,9},{9,10},{10,1... | collective-permute-start | bytes 786440 | tf_op jit(solution)/shard_map/ppermute | solution.py:51
  8.8 1.3 %collective-permute-start.1 = (bf16[128,1024]{1,0:T(8,128)(2,1)}, bf16[128,1024]{1,0:T(8,128)(2,1)}, u32[]{:S(2)}, u32[]{:S(2)}) collective-permute-start(bf16[128,1024]{1,0:T(8,128)(2,1)} %get-tuple-element.9), channel_id=1, source_target_pairs={{1,0},{2,1},{3,2},{4,3},{5,4},{6,5},{7,6},{8,7},{9,8},{10,9},{11,1... | collective-permute-start | bytes 786440 | tf_op jit(solution)/shard_map/ppermute | solution.py:53
  10.2 0.1 slice.75
  10.3 0.0 copy-start.3
  10.3 0.2 copy.66
  10.5 0.9 %reshape_reshape.3 = bf16[4,128,8,64]{1,0,3,2:T(4,128)(2,1)} reshape(bf16[512,512]{0,1:T(8,128)(2,1)S(1)} %copy.66) | data formatting | bytes 1048576 | tf_op jit(solution)/shard_map/reshape;reshape | solution.py:64
  11.5 0.9 %fusion.58 = (bf16[4,128,512]{2,1,0:T(8,128)(2,1)}, bf16[4,128,512]{2,1,0:T(8,128)(2,1)S(1)}) fusion(bf16[4,128,1024]{2,1,0:T(8,128)(2,1)S(1)} %bitcast.74), kind=kLoop, calls=%fused_computation.92 | loop fusion | bytes 2097152 | tf_op jit(solution)/shard_map/slice | solution.py:68
  12.4 0.0 copy-done.3
  12.4 1.0 %copy.68 = bf16[4,128,512]{1,2,0:T(8,128)(2,1)} copy(bf16[4,128,512]{2,1,0:T(8,128)(2,1)S(1)} %get-tuple-element.13) | data formatting | bytes 1048576 | tf_op jit(solution)/shard_map/slice | solution.py:67
  13.4 1.7 %bitcast_reduce_fusion.1 = (f32[4,128,8]{1,2,0:T(8,128)S(1)}, f32[4,8,128,128]{3,2,1,0:T(8,128)S(1)}) fusion(bf16[4,128,8,64]{1,3,2,0:T(8,128)(2,1)} %bitcast.81, bf16[4,128,8,64]{1,0,3,2:T(4,128)(2,1)} %reshape_reshape.3), kind=kOutput, calls=%fused_computation.6 | convolution fusion | flops 68153344 | bytes 3162112 | tf_op jit(solution)/shard_map/nqhd,nkhd->nqhk/dot_general | solution.py:80
  15.1 0.0 collective-permute-done.2
  15.2 0.0 copy-done.9
  15.2 4.3 %collective-permute-start.3 = (bf16[2,2,1024]{2,1,0:T(2,128)(2,1)S(1)}, bf16[2,2,1024]{2,1,0:T(2,128)(2,1)S(1)}, u32[]{:S(2)}, u32[]{:S(2)}) collective-permute-start(bf16[2,2,1024]{2,1,0:T(2,128)(2,1)S(1)} %pad_maximum_fusion.6), channel_id=1, source_target_pairs={{0,2},{1,3},{2,0},{3,1},{4,6},{5,7},{6,4},{7,5},{8,10},{9,11},{10,... | collective-permute-start | bytes 24584 | tf_op jit(solution)/shard_map/ppermute | solution.py:27
  19.5 0.0 copy-done.10
  19.5 1.6 %collective-permute-done.3 = bf16[2,2,1024]{2,1,0:T(2,128)(2,1)S(1)} collective-permute-done((bf16[2,2,1024]{2,1,0:T(2,128)(2,1)S(1)}, bf16[2,2,1024]{2,1,0:T(2,128)(2,1)S(1)}, u32[]{:S(2)}, u32[]{:S(2)}) %collective-permute-start.3) | collective-permute-done | bytes 8224 | tf_op jit(solution)/shard_map/ppermute | solution.py:27
  21.2 3.0 %collective-permute-start.4 = (bf16[4,2,1024]{2,1,0:T(2,128)(2,1)S(1)}, bf16[4,2,1024]{2,1,0:T(2,128)(2,1)S(1)}, u32[]{:S(2)}, u32[]{:S(2)}) collective-permute-start(bf16[4,2,1024]{2,1,0:T(2,128)(2,1)S(1)} %pad_maximum_fusion.5), channel_id=1, source_target_pairs={{0,4},{1,5},{2,6},{3,7},{4,0},{5,1},{6,2},{7,3},{8,12},{9,13},{10,... | collective-permute-start | bytes 49160 | tf_op jit(solution)/shard_map/ppermute | solution.py:27
  24.2 0.0 copy-done.11
  24.2 1.7 %collective-permute-done.4 = bf16[4,2,1024]{2,1,0:T(2,128)(2,1)S(1)} collective-permute-done((bf16[4,2,1024]{2,1,0:T(2,128)(2,1)S(1)}, bf16[4,2,1024]{2,1,0:T(2,128)(2,1)S(1)}, u32[]{:S(2)}, u32[]{:S(2)}) %collective-permute-start.4) | collective-permute-done | bytes 16416 | tf_op jit(solution)/shard_map/ppermute | solution.py:27
  26.0 3.1 %collective-permute-start.5 = (bf16[8,2,1024]{2,1,0:T(2,128)(2,1)S(1)}, bf16[8,2,1024]{2,1,0:T(2,128)(2,1)S(1)}, u32[]{:S(2)}, u32[]{:S(2)}) collective-permute-start(bf16[8,2,1024]{2,1,0:T(2,128)(2,1)S(1)} %pad_maximum_fusion.4), channel_id=1, source_target_pairs={{0,8},{1,9},{2,10},{3,11},{4,12},{5,13},{6,14},{7,15},{8,0},{9,1},... | collective-permute-start | bytes 98312 | tf_op jit(solution)/shard_map/ppermute | solution.py:27
  29.1 2.0 %copy.76 = bf16[4,128,512]{1,2,0:T(8,128)(2,1)} copy(bf16[4,128,512]{2,1,0:T(8,128)(2,1)} %get-tuple-element.12) | data formatting | bytes 1048576 | tf_op jit(solution)/shard_map/slice | solution.py:68
  31.2 0.0 collective-permute-done.5
  31.2 0.1 broadcast_select_fusion.3
  31.3 0.1 pad_maximum_fusion.3
  31.4 4.4 %collective-permute-start.6 = (bf16[16,2,1024]{2,1,0:T(2,128)(2,1)S(1)}, bf16[16,2,1024]{2,1,0:T(2,128)(2,1)S(1)}, u32[]{:S(2)}, u32[]{:S(2)}) collective-permute-start(bf16[16,2,1024]{2,1,0:T(2,128)(2,1)S(1)} %pad_maximum_fusion.3), channel_id=1, source_target_pairs={{0,16},{1,17},{2,18},{3,19},{4,20},{5,21},{6,22},{7,23},{8,24},{9,... | collective-permute-start | bytes 196616 | tf_op jit(solution)/shard_map/ppermute | solution.py:27
  35.8 2.2 %collective-permute-done.6 = bf16[16,2,1024]{2,1,0:T(2,128)(2,1)S(1)} collective-permute-done((bf16[16,2,1024]{2,1,0:T(2,128)(2,1)S(1)}, bf16[16,2,1024]{2,1,0:T(2,128)(2,1)S(1)}, u32[]{:S(2)}, u32[]{:S(2)}) %collective-permute-start.6) | collective-permute-done | bytes 65568 | tf_op jit(solution)/shard_map/ppermute | solution.py:27
  38.0 0.1 broadcast_select_fusion.1
  38.2 0.2 pad_maximum_fusion.2
  38.4 0.1 reshape.90
  38.4 0.6 gather_fusion
  39.1 2.1 %fusion.16 = bf16[32,1024]{1,0:T(8,128)(2,1)S(1)} fusion(bf16[1024,1536]{1,0:T(8,128)(2,1)} %param.6, bf16[32,1024]{1,0:T(8,128)(2,1)S(1)} %gather_fusion, pred[32]{0:T(512)(128)(4,1)S(1)} %compare_and_fusion), kind=kOutput, calls=%fused_computation.30 | convolution fusion | flops 67174400 | bytes 2228256 | tf_op jit(solution)/shard_map/dot_general | solution.py:148
  41.2 0.1 reshape.91
  41.3 0.1 reshape.94
  41.4 2.1 %fusion.61 = (f32[4,128,8]{1,0,2:T(4,128)S(1)}, f32[4,128,8,32]{1,3,0,2:T(8,128)}) fusion(bf16[4,128,8,64]{1,0,3,2:T(4,128)(2,1)} %reshape_reshape.3, bf16[32,8,64,1]{2,1,0,3:T(8,128)(2,1)S(1)} %bitcast.83), kind=kOutput, calls=%fused_computation.95 | convolution fusion | flops 17035264 | bytes 1097728 | tf_op jit(solution)/shard_map/nqhd,chd->nqhc/dot_general | solution.py:92
  43.4 0.0 collective-permute-done
  43.5 0.0 collective-permute-done.1
  43.5 2.7 %pad_maximum_fusion.1 = (bf16[512,1024]{1,0:T(8,128)(2,1)S(1)}, bf16[512,1024]{1,0:T(8,128)(2,1)}) fusion(bf16[512,1024]{1,0:T(8,128)(2,1)} %copy-done.3, bf16[128,1024]{1,0:T(8,128)(2,1)} %collective-permute-done, bf16[128,1024]{1,0:T(8,128)(2,1)} %collective-permute-done.1), kind=kLoop, calls=%fused_computation.33 | loop fusion | flops 4194304 | bytes 3670016 | tf_op jit(solution)/shard_map/concatenate | solution.py:49
  46.1 1.1 %fusion.59 = (bf16[4,128,512]{2,1,0:T(8,128)(2,1)}, bf16[4,128,512]{2,1,0:T(8,128)(2,1)}) fusion(bf16[4,128,1024]{2,1,0:T(8,128)(2,1)S(1)} %bitcast.76), kind=kLoop, calls=%fused_computation.93 | loop fusion | bytes 2097152 | tf_op jit(solution)/shard_map/slice | solution.py:68
  47.3 2.0 %copy.65 = bf16[4,128,512]{1,2,0:T(8,128)(2,1)} copy(bf16[4,128,512]{2,1,0:T(8,128)(2,1)} %get-tuple-element.15) | data formatting | bytes 1048576 | tf_op jit(solution)/shard_map/slice | solution.py:67
  49.3 2.2 %fusion.57 = (bf16[4,128,512]{2,1,0:T(8,128)(2,1)}, bf16[4,128,512]{2,1,0:T(8,128)(2,1)}) fusion(bf16[4,128,1024]{2,1,0:T(8,128)(2,1)} %bitcast.75), kind=kLoop, calls=%fused_computation.91 | loop fusion | bytes 2097152 | tf_op jit(solution)/shard_map/slice | solution.py:68
  51.5 2.1 %copy.70 = bf16[4,128,512]{1,2,0:T(8,128)(2,1)} copy(bf16[4,128,512]{2,1,0:T(8,128)(2,1)} %get-tuple-element.11) | data formatting | bytes 1048576 | tf_op jit(solution)/shard_map/slice | solution.py:67
  53.6 3.2 %bitcast_reduce_fusion.2 = (f32[4,128,8]{1,2,0:T(8,128)S(1)}, f32[4,8,128,128]{3,2,1,0:T(8,128)}) fusion(pred[4]{0:T(512)(128)(4,1)S(1)} %get-tuple-element.32, bf16[4,128,8,64]{1,3,2,0:T(8,128)(2,1)} %bitcast.78, bf16[4,128,8,64]{1,0,3,2:T(4,128)(2,1)} %reshape_reshape.3), kind=kOutput, calls=%fused_computation.9 | convolution fusion | flops 68677632 | bytes 3162116 | tf_op jit(solution)/shard_map/nqhd,nkhd->nqhk/dot_general | solution.py:80
  56.9 0.0 copy-done.2
  56.9 0.0 copy-done.7
  56.9 2.0 %bitcast_reduce_fusion = (f32[4,128,8]{1,2,0:T(8,128)S(1)}, f32[4,8,128,128]{3,2,1,0:T(8,128)}) fusion(pred[4]{0:T(512)(128)(4,1)S(1)} %get-tuple-element.33, bf16[4,128,8,64]{1,3,2,0:T(8,128)(2,1)S(1)} %bitcast.79, bf16[4,128,8,64]{1,0,3,2:T(4,128)(2,1)S(1)} %copy-done.2), kind=kOutput, calls=%fused_computation.3 | convolution fusion | flops 68677632 | bytes 3162116 | tf_op jit(solution)/shard_map/nqhd,nkhd->nqhk/dot_general | solution.py:80
  58.9 2.0 %copy.64 = bf16[4,128,512]{1,2,0:T(8,128)(2,1)} copy(bf16[4,128,512]{2,1,0:T(8,128)(2,1)} %get-tuple-element.14) | data formatting | bytes 1048576 | tf_op jit(solution)/shard_map/slice | solution.py:68
  60.9 2.1 %copy.78 = bf16[4,128,512]{1,2,0:T(8,128)(2,1)} copy(bf16[4,128,512]{2,1,0:T(8,128)(2,1)} %get-tuple-element.10) | data formatting | bytes 1048576 | tf_op jit(solution)/shard_map/slice | solution.py:68
  63.0 2.6 %fusion.20 = f32[4,8,64,128]{3,2,1,0:T(8,128)S(1)} fusion(bf16[4,128,8,64]{1,3,2,0:T(8,128)(2,1)} %bitcast.80, f32[4,8,128,128]{3,2,1,0:T(8,128)} %get-tuple-element.39, f32[4,128,8]{1,2,0:T(8,128)S(1)} %fusion.49, pred[4]{0:T(512)(128)(4,1)S(1)} %get-tuple-element.32), kind=kOutput, calls=%fused_computation.31 | convolution fusion | flops 69206016 | bytes 3686404 | tf_op jit(solution)/shard_map/nqhk,nkhd->nqhd/dot_general | solution.py:117
  65.6 0.0 copy-done.1
  65.6 0.0 copy-start.6
  65.6 3.2 %fusion.5 = (f32[4,128,8]{1,2,0:T(8,128)S(1)}, f32[4,128,8]{1,2,0:T(8,128)S(1)}, f32[4,128,8]{1,2,0:T(8,128)S(1)}) fusion(f32[4,8,128,128]{3,2,1,0:T(8,128)S(1)} %get-tuple-element.41, f32[4,128,8]{1,2,0:T(8,128)S(1)} %fusion.49, f32[4,8,128,128]{3,2,1,0:T(8,128)S(1)} %copy-done.1, pred[4]{0:T(512)(128)(4,1)S(1)} %get-tuple-element.32, ...), kind=kLoop, calls=%fused_computation.15 | loop fusion | flops 5754880 | bytes 6357000 | tf_op jit(solution)/shard_map/reduce_sum | solution.py:111
  68.8 0.1 fusion.34
  69.0 0.0 copy-done.5
  69.0 0.5 convolution_add_fusion.1
  69.5 0.3 convolution_bitcast_fusion
  69.9 0.7 copy-done.4
  70.6 0.1 copy-done.8
  70.7 0.8 %fusion.14 = bf16[4,128,8,64]{1,3,2,0:T(8,128)(2,1)S(1)} fusion(f32[4,128,8,64]{1,3,2,0:T(8,128)S(1)} %convolution_bitcast_fusion, f32[4,8,64,128]{3,2,1,0:T(8,128)S(1)} %convolution_add_fusion.1, bf16[4,128,8,64]{1,3,2,0:T(8,128)(2,1)S(1)} %bitcast.82, f32[4,8,128,128]{3,2,1,0:T(8,128)S(1)} %copy-done.4, f32[4,128,8]{1,2,0:T(8,128)S(1)} %fusion.49, ...), kind=kOutput, calls=%fused_computation.27 | convolution fusion | flops 70254592 | bytes 5275652 | tf_op jit(solution)/shard_map/nqhk,nkhd->nqhd/dot_general | solution.py:117
  71.5 0.6 copy.92
  72.0 1.4 %reshape.107 = bf16[512,512]{1,0:T(8,128)(2,1)} reshape(bf16[4,128,8,64]{3,2,1,0:T(8,128)(2,1)S(1)} %copy.92) | data formatting | bytes 1048576 | tf_op jit(solution)/shard_map/reshape | solution.py:133
  (25 shorter events, 0.3 us)
Async XLA Ops:
  0.0 1.2 %copy-start = (bf16[512,1024]{1,0:T(8,128)(2,1)S(1)}, bf16[512,1024]{1,0:T(8,128)(2,1)}, u32[]{:S(2)}) copy-start(bf16[512,1024]{1,0:T(8,128)(2,1)} %param.5) | copy-start | bytes 3145732
  0.0 15.1 %collective-permute-start.2 = (bf16[1,2,1024]{2,1,0:T(2,128)(2,1)}, bf16[1,2,1024]{2,1,0:T(2,128)(2,1)S(1)}, u32[]{:S(2)}, u32[]{:S(2)}) collective-permute-start(bf16[1,2,1024]{2,1,0:T(2,128)(2,1)} %bitcast.84), channel_id=1, source_target_pairs={{0,1},{1,0},{2,3},{3,2},{4,5},{5,4},{6,7},{7,6},{8,9},{9,8},{10,11... | collective-permute-start | bytes 12296 | tf_op jit(solution)/shard_map/ppermute | solution.py:27
  5.8 37.7 %collective-permute-start = (bf16[128,1024]{1,0:T(8,128)(2,1)}, bf16[128,1024]{1,0:T(8,128)(2,1)}, u32[]{:S(2)}, u32[]{:S(2)}) collective-permute-start(bf16[128,1024]{1,0:T(8,128)(2,1)} %get-tuple-element.8), channel_id=1, source_target_pairs={{0,1},{1,2},{2,3},{3,4},{4,5},{5,6},{6,7},{7,8},{8,9},{9,10},{10,1... | collective-permute-start | bytes 786440 | tf_op jit(solution)/shard_map/ppermute | solution.py:51
  8.8 34.6 %collective-permute-start.1 = (bf16[128,1024]{1,0:T(8,128)(2,1)}, bf16[128,1024]{1,0:T(8,128)(2,1)}, u32[]{:S(2)}, u32[]{:S(2)}) collective-permute-start(bf16[128,1024]{1,0:T(8,128)(2,1)} %get-tuple-element.9), channel_id=1, source_target_pairs={{1,0},{2,1},{3,2},{4,3},{5,4},{6,5},{7,6},{8,7},{9,8},{10,9},{11,1... | collective-permute-start | bytes 786440 | tf_op jit(solution)/shard_map/ppermute | solution.py:53
  10.3 2.1 %copy-start.3 = (bf16[512,1024]{1,0:T(8,128)(2,1)}, bf16[512,1024]{1,0:T(8,128)(2,1)S(1)}, u32[]{:S(2)}) copy-start(bf16[512,1024]{1,0:T(8,128)(2,1)S(1)} %slice.75) | copy-start | bytes 3145732
  12.4 2.8 %copy-start.9 = (bf16[2,1024]{1,0:T(2,128)(2,1)S(1)}, bf16[2,1024]{1,0:T(2,128)(2,1)}, u32[]{:S(2)}) copy-start(bf16[2,1024]{1,0:T(2,128)(2,1)} %param.7) | copy-start | bytes 12292
  12.4 7.1 %copy-start.10 = (s32[4,2]{0,1:T(2,128)S(1)}, s32[4,2]{0,1:T(2,128)}, u32[]{:S(2)}) copy-start(s32[4,2]{0,1:T(2,128)} %param.9) | copy-start | bytes 100
  12.4 11.8 %copy-start.11 = (s32[32]{0:T(128)S(1)}, s32[32]{0:T(128)}, u32[]{:S(2)}) copy-start(s32[32]{0:T(128)} %param.8) | copy-start | bytes 388
  15.2 5.9 %collective-permute-start.3 = (bf16[2,2,1024]{2,1,0:T(2,128)(2,1)S(1)}, bf16[2,2,1024]{2,1,0:T(2,128)(2,1)S(1)}, u32[]{:S(2)}, u32[]{:S(2)}) collective-permute-start(bf16[2,2,1024]{2,1,0:T(2,128)(2,1)S(1)} %pad_maximum_fusion.6), channel_id=1, source_target_pairs={{0,2},{1,3},{2,0},{3,1},{4,6},{5,7},{6,4},{7,5},{8,10},{9,11},{10,... | collective-permute-start | bytes 24584 | tf_op jit(solution)/shard_map/ppermute | solution.py:27
  21.2 4.8 %collective-permute-start.4 = (bf16[4,2,1024]{2,1,0:T(2,128)(2,1)S(1)}, bf16[4,2,1024]{2,1,0:T(2,128)(2,1)S(1)}, u32[]{:S(2)}, u32[]{:S(2)}) collective-permute-start(bf16[4,2,1024]{2,1,0:T(2,128)(2,1)S(1)} %pad_maximum_fusion.5), channel_id=1, source_target_pairs={{0,4},{1,5},{2,6},{3,7},{4,0},{5,1},{6,2},{7,3},{8,12},{9,13},{10,... | collective-permute-start | bytes 49160 | tf_op jit(solution)/shard_map/ppermute | solution.py:27
  26.0 5.1 %collective-permute-start.5 = (bf16[8,2,1024]{2,1,0:T(2,128)(2,1)S(1)}, bf16[8,2,1024]{2,1,0:T(2,128)(2,1)S(1)}, u32[]{:S(2)}, u32[]{:S(2)}) collective-permute-start(bf16[8,2,1024]{2,1,0:T(2,128)(2,1)S(1)} %pad_maximum_fusion.4), channel_id=1, source_target_pairs={{0,8},{1,9},{2,10},{3,11},{4,12},{5,13},{6,14},{7,15},{8,0},{9,1},... | collective-permute-start | bytes 98312 | tf_op jit(solution)/shard_map/ppermute | solution.py:27
  31.4 6.7 %collective-permute-start.6 = (bf16[16,2,1024]{2,1,0:T(2,128)(2,1)S(1)}, bf16[16,2,1024]{2,1,0:T(2,128)(2,1)S(1)}, u32[]{:S(2)}, u32[]{:S(2)}) collective-permute-start(bf16[16,2,1024]{2,1,0:T(2,128)(2,1)S(1)} %pad_maximum_fusion.3), channel_id=1, source_target_pairs={{0,16},{1,17},{2,18},{3,19},{4,20},{5,21},{6,22},{7,23},{8,24},{9,... | collective-permute-start | bytes 196616 | tf_op jit(solution)/shard_map/ppermute | solution.py:27
  53.6 3.2 %copy-start.2 = (bf16[4,128,8,64]{1,0,3,2:T(4,128)(2,1)S(1)}, bf16[4,128,8,64]{1,0,3,2:T(4,128)(2,1)}, u32[]{:S(2)}) copy-start(bf16[4,128,8,64]{1,0,3,2:T(4,128)(2,1)} %reshape_reshape.3) | copy-start | bytes 1572868
  53.6 3.2 %copy-start.7 = (bf16[4,128,512]{1,2,0:T(8,128)(2,1)S(1)}, bf16[4,128,512]{1,2,0:T(8,128)(2,1)}, u32[]{:S(2)}) copy-start(bf16[4,128,512]{1,2,0:T(8,128)(2,1)} %copy.70) | copy-start | bytes 1572868
  63.0 2.6 %copy-start.1 = (f32[4,8,128,128]{3,2,1,0:T(8,128)S(1)}, f32[4,8,128,128]{3,2,1,0:T(8,128)}, u32[]{:S(2)}) copy-start(f32[4,8,128,128]{3,2,1,0:T(8,128)} %get-tuple-element.39) | copy-start | bytes 6291460
  65.6 3.2 %copy-start.6 = (f32[4,128,8,32]{1,3,0,2:T(8,128)S(1)}, f32[4,128,8,32]{1,3,0,2:T(8,128)}, u32[]{:S(2)}) copy-start(f32[4,128,8,32]{1,3,0,2:T(8,128)} %get-tuple-element.37) | copy-start | bytes 1572868
  65.6 3.4 %copy-start.5 = (bf16[4,128,512]{1,2,0:T(8,128)(2,1)S(1)}, bf16[4,128,512]{1,2,0:T(8,128)(2,1)}, u32[]{:S(2)}) copy-start(bf16[4,128,512]{1,2,0:T(8,128)(2,1)} %copy.76) | copy-start | bytes 1572868
  69.0 1.6 %copy-start.4 = (f32[4,8,128,128]{3,2,1,0:T(8,128)S(1)}, f32[4,8,128,128]{3,2,1,0:T(8,128)}, u32[]{:S(2)}) copy-start(f32[4,8,128,128]{3,2,1,0:T(8,128)} %get-tuple-element.35) | copy-start | bytes 6291460
  69.0 1.7 %copy-start.8 = (bf16[4,128,512]{1,2,0:T(8,128)(2,1)S(1)}, bf16[4,128,512]{1,2,0:T(8,128)(2,1)}, u32[]{:S(2)}) copy-start(bf16[4,128,512]{1,2,0:T(8,128)(2,1)} %copy.78) | copy-start | bytes 1572868
